TPU v7x, 32 devices: a whole 2x2x4 slice. The times are simulated.
32 devices in a mesh: seq: 32 (over z, y, x, core).
Axes of the slice: x: 2, y: 2, z: 4, core: 2. Of those that a mesh axis runs over, the one named last changes fastest.
Arguments:
- acceptance_gate: bfloat16 [4096, 2048], P('seq'), may hold values from -1.1953125 to 1.1953125
- lookup_matrix: bfloat16 [4096, 2048], P('seq'), may hold values from -0.29882812 to 0.29882812
- payload_matrix: bfloat16 [4096, 2048], P('seq'), may hold values from -6 to 6
- fading_parameter: float32 [4096, 2048], P('seq'), may hold values from -17 to 0.5
- present_reward: float32 [2048], replicated, may hold values from -4 to 4
- emitted_cotangent: bfloat16 [4096, 2048], P('seq'), may hold values from -0.119628906 to 0.119628906
- paper_spans: int32 [64], replicated, may hold values from 1 to 1024, 4096 in all
Outputs:
- grad_receptance: bfloat16 [4096, 2048], P('seq')
- grad_key: bfloat16 [4096, 2048], P('seq')
- grad_value: bfloat16 [4096, 2048], P('seq')
- grad_decay: bfloat16 [4096, 2048], P('seq')
- reward_cotangent: float32 [2048], replicated
Inputs may be any that keep to these rules, and one draw needn't show every extreme that they name: `paper_spans`: the 64 documents fill the packed sequence of 4096 tokens in order.
All inputs are finite; a program needn't handle non-finite values.
Results may differ from a plain program's by a relative error of at most 0.001.
Values sent between devices are 32-bit elements; how exact they have to be, the bound alone decides.
A program may use at most 320 MiB of HBM per device.

v0:
```python
import functools

import jax
import jax.numpy as jnp
from jax import lax
from jax.experimental import pallas as pl
from jax.experimental.pallas import tpu as pltpu
from jax.sharding import PartitionSpec as P

HS = 64
LANES = 128
HALF = 32
BLOCK_ROWS = 72
GROUPS = 4
MESH = pl.DeviceIdType.MESH
F32 = jnp.float32
BF16 = jnp.bfloat16


def split2(x):
    hi = x.astype(BF16)
    lo = (x - hi.astype(F32)).astype(BF16)
    return hi, lo


def split3(x):
    hi = x.astype(BF16)
    rest = x - hi.astype(F32)
    mid = rest.astype(BF16)
    lo = (rest - mid.astype(F32)).astype(BF16)
    return hi, mid, lo


def lanes(*xs):
    return jnp.concatenate(xs, axis=1)


def rows(*xs):
    return jnp.concatenate(xs, axis=0)


def dot(a, b):
    return lax.dot_general(a, b, (((1,), (0,)), ((), ())), preferred_element_type=F32)


def dot_nt(a, b):
    return lax.dot_general(a, b, (((1,), (1,)), ((), ())), preferred_element_type=F32)


def kernel(
    n,
    r_ref,
    k_ref,
    v_ref,
    x_ref,
    u_ref,
    dy_ref,
    spans_ref,
    dr_ref,
    dk_ref,
    dv_ref,
    dx_ref,
    du_ref,
    lw_s,
    cum_s,
    dyv_s,
    dq_s,
    dkk_s,
    dvv_s,
    mask_s,
    maskt_s,
    carried_s,
    keep_s,
    flag_s,
    blk,
    rx1,
    tx2,
    rx2,
    tot,
    rx3f,
    rx3b,
    rx3t,
    tx4,
    rx4,
    tx5,
    fin,
    core_send,
    core_recv,
    send2,
    recv2,
    send3,
    recv3,
    send3t,
    recv3t,
    send4,
    recv4,
):
    tokens, width = r_ref.shape
    pairs = width // LANES
    group_size = n // GROUPS
    chips = group_size // 2
    piece = width // chips
    me = lax.axis_index("seq")
    core = lax.rem(me, 2)
    chip = lax.rem(me // 2, chips)
    group = me // group_size
    partner = me + 1 - 2 * core

    def at_chip(offset):
        target = lax.rem(chip + offset, chips)
        return target, group * group_size + target * 2 + core

    def at_group(offset):
        return lax.rem(group + offset, GROUPS) * group_size + chip * 2 + core

    barrier = pltpu.get_barrier_semaphore()
    friends = [partner]
    friends += [at_chip(o)[1] for o in range(1, chips)]
    friends += [at_group(o) for o in range(1, GROUPS)]
    for friend in friends:
        pl.semaphore_signal(barrier, inc=1, device_id=(friend,), device_id_type=MESH)

    docs = spans_ref.shape[1]
    spans_row = spans_ref[...].astype(F32)
    one = lax.broadcasted_iota(jnp.int32, (docs, docs), 0)
    two = lax.broadcasted_iota(jnp.int32, (docs, docs), 1)
    spread = jnp.broadcast_to(spans_row, (docs, docs))
    spans_col = jnp.sum(jnp.where(one == two, spread, 0.0), axis=1, keepdims=True)
    starts_col = jnp.sum(jnp.where(two < one, spread, 0.0), axis=1, keepdims=True)
    starts_row = jnp.sum(jnp.where(one < two, spans_col, 0.0), axis=0, keepdims=True)
    base = (me * tokens).astype(F32)
    pos_col = base + lax.broadcasted_iota(jnp.int32, (tokens, 1), 0).astype(F32)
    pos_row = base + lax.broadcasted_iota(jnp.int32, (1, tokens), 1).astype(F32)
    seg_col = jnp.sum((starts_row <= pos_col).astype(F32), axis=1, keepdims=True)
    seg_row = jnp.sum((starts_col <= pos_row).astype(F32), axis=0, keepdims=True)
    seg_prev = jnp.sum((starts_row <= base - 1.0).astype(F32), axis=1, keepdims=True)
    seg_last = jnp.sum(
        (starts_row <= base + (tokens - 1.0)).astype(F32), axis=1, keepdims=True
    )
    first = lax.broadcasted_iota(jnp.int32, (tokens, tokens), 0)
    second = lax.broadcasted_iota(jnp.int32, (tokens, tokens), 1)
    same = seg_col == seg_row
    mask = jnp.where((first > second) & same, 1.0, 0.0)
    maskt = jnp.where((second > first) & same, 1.0, 0.0)
    mask_s[...] = rows(mask, mask)
    maskt_s[...] = rows(maskt, maskt)
    carried_s[...] = jnp.broadcast_to((seg_col == seg_prev).astype(F32), (tokens, LANES))
    keep_s[...] = jnp.broadcast_to((seg_col == seg_last).astype(F32), (tokens, LANES))
    flag_s[...] = jnp.broadcast_to((seg_last == seg_prev).astype(F32), (8, LANES))

    lane = lax.broadcasted_iota(jnp.int32, (1, LANES), 1)
    in_a = lane < HS
    mask_a = in_a.astype(F32).astype(BF16)
    mask_b = (1.0 - in_a.astype(F32)).astype(BF16)
    lower = jnp.where(first >= second, 1.0, 0.0).astype(BF16)
    upper = jnp.where(first <= second, 1.0, 0.0).astype(BF16)
    lower3 = lanes(lower, lower, lower)
    upper3 = lanes(upper, upper, upper)
    head_i = lax.broadcasted_iota(jnp.int32, (LANES, LANES), 0) // HS
    head_j = lax.broadcasted_iota(jnp.int32, (LANES, LANES), 1) // HS
    ones = jnp.where(head_i == head_j, 1.0, 0.0).astype(BF16)
    ones2 = rows(ones, ones)
    ones3 = rows(ones, ones, ones)

    def stacked(x):
        return rows(x * mask_a, x * mask_b)

    def pick(x):
        m = x.shape[0] // 2
        return jnp.where(in_a, x[:m], x[m:])

    def where_of(p):
        cols = pl.ds(pl.multiple_of(p * LANES, LANES), LANES)
        per = piece // LANES
        sub = pl.ds(pl.multiple_of(lax.rem(p, per) * LANES, LANES), LANES)
        return cols, p // per, sub

    def summarise(p):
        cols, slot, sub = where_of(p)
        r, k = r_ref[:, cols].astype(F32), k_ref[:, cols].astype(F32)
        v, dy = v_ref[:, cols], dy_ref[:, cols]
        lw = -jnp.exp(x_ref[:, cols])
        cum = dot(lower3, rows(*split3(lw)))
        lw_s[:, cols] = lw
        cum_s[:, cols] = cum
        last = cum[tokens - 1 : tokens]
        ending = k * jnp.exp(last - cum) * keep_s[...]
        reached = r * jnp.exp(cum - lw) * carried_s[...]
        vt, dyt = v.T, dy.T
        ends = pick(dot(lanes(vt, vt), rows(*split2(ending))))
        pulls = pick(dot(lanes(dyt, dyt), rows(*split2(reached))))
        dyv = dot(lanes(*split2(dy.astype(F32) * v.astype(F32))), ones2)
        dyv_s[:, cols] = dyv
        du = jnp.sum(dyv * r * k, axis=0, keepdims=True)
        through = jnp.exp(last) * flag_s[0:1]
        tail = rows(through, du, jnp.zeros((6, LANES), F32))
        for h in range(2):
            blk[h, slot, 0:HALF, sub] = ends[h * HALF : (h + 1) * HALF]
            blk[h, slot, HALF : 2 * HALF, sub] = pulls[h * HALF : (h + 1) * HALF]
            blk[h, slot, 2 * HALF : BLOCK_ROWS, sub] = tail

    def local_part(p):
        cols, _, _ = where_of(p)
        r, k = r_ref[:, cols].astype(F32), k_ref[:, cols].astype(F32)
        v, dy = v_ref[:, cols], dy_ref[:, cols]
        lw, cum = lw_s[:, cols], cum_s[:, cols]
        qh, ql = split2(r * jnp.exp(cum - lw))
        kh, kl = split2(k * jnp.exp(-cum))
        kh2, kl2 = stacked(kh), stacked(kl)
        at = dot_nt(lanes(kh2, kl2, kh2), lanes(qh, qh, ql))
        at = jnp.where(maskt_s[...] > 0.0, at, 0.0)
        da = jnp.where(mask_s[...] > 0.0, dot_nt(stacked(dy), v), 0.0)
        dat = jnp.where(maskt_s[...] > 0.0, dot_nt(stacked(v), dy), 0.0)
        dvv_s[:, cols] = pick(dot(lanes(*split2(at)), rows(dy, dy)))
        dah, dal = split2(da)
        dq_s[:, cols] = pick(dot(lanes(dah, dal, dah), rows(kh, kh, kl)))
        dth, dtl = split2(dat)
        dkk_s[:, cols] = pick(dot(lanes(dth, dtl, dth), rows(qh, qh, ql)))

    def finish(p):
        cols, slot, sub = where_of(p)
        r, k = r_ref[:, cols].astype(F32), k_ref[:, cols].astype(F32)
        v, dy = v_ref[:, cols], dy_ref[:, cols]
        u = u_ref[:, cols]
        lw, cum, dyv = lw_s[:, cols], cum_s[:, cols], dyv_s[:, cols]
        s = rows(fin[0, slot, 0:HALF, sub], fin[1, slot, 0:HALF, sub])
        g = rows(fin[0, slot, HALF : 2 * HALF, sub], fin[1, slot, HALF : 2 * HALF, sub])
        sh, sl = split2(rows(jnp.where(in_a, s, 0.0), jnp.where(in_a, 0.0, s)))
        gh, gl = split2(rows(jnp.where(in_a, g, 0.0), jnp.where(in_a, 0.0, g)))
        dq = dq_s[:, cols] + dot(lanes(dy, dy), rows(sh, sl)) * carried_s[...]
        de = dot(lanes(v, v), rows(gh, gl))
        last = cum[tokens - 1 : tokens]
        fade = jnp.exp(last - cum) * keep_s[...]
        ending = k * fade
        eh, el = split2(ending)
        eb, enc = jnp.exp(cum - lw), jnp.exp(-cum)
        bonus = dot(lanes(*split3(r * u * k)), ones3)
        dkk = dkk_s[:, cols]
        dv = dvv_s[:, cols] + dot_nt(lanes(eh, el, eh), lanes(gh, gh, gl))
        dv = dv + bonus * dy.astype(F32)
        du = dyv * u
        dr_ref[:, cols] = (dq * eb + du * k).astype(BF16)
        dk_ref[:, cols] = (dkk * enc + de * fade + du * r).astype(BF16)
        dv_ref[:, cols] = dv.astype(BF16)
        db = dq * (r * eb)
        ee = de * ending
        through = jnp.exp(last) * flag_s[0:1]
        tail = jnp.sum(ee, axis=0, keepdims=True)
        tail = tail + through * jnp.sum(s * g, axis=0, keepdims=True)
        total = db - dkk * (k * enc) - ee
        rev = dot(upper3, rows(*split3(total))) + tail - db
        dx_ref[:, cols] = (rev * lw).astype(BF16)
        du_ref[:, cols] = fin[0, slot, 2 * HALF + 1 : 2 * HALF + 2, sub]

    def run(part, low, high):
        def step(i, carry):
            part(2 * i)
            part(2 * i + 1)
            return carry

        lax.fori_loop(low, high, step, 0)

    cuts = [pairs * c // 16 for c in (0, 1, 4, 5, 7, 8)]
    run(summarise, 0, pairs // 2)

    def remote(src, dst, send, recv, device):
        return pltpu.make_async_remote_copy(
            src_ref=src,
            dst_ref=dst,
            send_sem=send,
            recv_sem=recv,
            device_id=(device,),
            device_id_type=MESH,
        )

    pl.semaphore_wait(barrier, len(friends))

    copy1 = remote(blk.at[1 - core], rx1, core_send.at[0], core_recv.at[0], partner)
    copy1.start()
    run(local_part, cuts[0], cuts[1])
    copy1.wait_recv()
    late = core == 1
    e_rows, p_rows = slice(0, HALF), slice(HALF, 2 * HALF)
    t_row, u_row = slice(2 * HALF, 2 * HALF + 1), slice(2 * HALF + 1, 2 * HALF + 2)
    end_rows = slice(2 * HALF, BLOCK_ROWS)

    def tail_of(t, u):
        return rows(t, u, jnp.zeros((6, piece), F32))

    def combine(c, carry):
        ta, tb = blk[core, c, t_row], rx1[c, t_row]
        ea, eb = blk[core, c, e_rows], rx1[c, e_rows]
        pa, pb = blk[core, c, p_rows], rx1[c, p_rows]
        tx2[c, e_rows] = jnp.where(late, ta * eb + ea, tb * ea + eb)
        tx2[c, p_rows] = jnp.where(late, pb + tb * pa, pa + ta * pb)
        tx2[c, end_rows] = tail_of(ta * tb, blk[core, c, u_row] + rx1[c, u_row])
        return carry

    lax.fori_loop(0, chips, combine, 0)

    copies2 = []
    for o in range(1, chips):
        target, device = at_chip(o)
        copies2.append(
            remote(tx2.at[target], rx2.at[chip], send2.at[o], recv2.at[o], device)
        )
        copies2[-1].start()
    rx2[chip] = tx2[chip]
    run(local_part, cuts[1], cuts[2])
    for copy in copies2:
        copy.wait_recv()

    def forward(c, carry):
        f, t, du = carry
        tx4[c, e_rows] = f
        tc = rx2[c, t_row]
        tx4[c, t_row] = t
        return tc * f + rx2[c, e_rows], t * tc, du + rx2[c, u_row]

    zero, row = jnp.zeros((HALF, piece), F32), jnp.zeros((1, piece), F32)
    f, t, du = lax.fori_loop(0, chips, forward, (zero, row + 1.0, row))

    def backward(i, carry):
        c = chips - 1 - i
        b, t = carry
        tx4[c, p_rows] = b
        tc = rx2[c, t_row]
        tx4[c, u_row] = t
        return rx2[c, p_rows] + tc * b, t * tc

    b, t = lax.fori_loop(0, chips, backward, (zero, row + 1.0))
    tot[e_rows] = f
    tot[p_rows] = b
    tot[end_rows] = tail_of(t, du)

    ahead = remote(tot.at[e_rows], rx3f, send3.at[0], recv3.at[0], at_group(1))
    behind = remote(
        tot.at[p_rows], rx3b, send3.at[1], recv3.at[1], at_group(GROUPS - 1)
    )
    has_next, has_prev = group < GROUPS - 1, group > 0

    @pl.when(has_next)
    def _():
        ahead.start()

    @pl.when(has_prev)
    def _():
        behind.start()

    copies3 = []
    for o in range(1, GROUPS):
        copies3.append(
            remote(
                tot.at[end_rows],
                rx3t.at[o - 1],
                send3t.at[o - 1],
                recv3t.at[o - 1],
                at_group(o),
            )
        )
        copies3[-1].start()
    run(local_part, cuts[2], cuts[3])

    @pl.when(has_prev)
    def _():
        ahead.wait_recv()

    @pl.when(jnp.logical_not(has_prev))
    def _():
        rx3f[...] = zero

    @pl.when(has_next)
    def _():
        behind.wait_recv()

    @pl.when(jnp.logical_not(has_next))
    def _():
        rx3b[...] = zero

    for copy in copies3:
        copy.wait_recv()
    du = tot[u_row]
    for o in range(1, GROUPS):
        du = du + rx3t[o - 1, 1:2]

    def carry_in(c, carry):
        tx4[c, e_rows] = tx4[c, e_rows] + tx4[c, t_row] * rx3f[...]
        tx4[c, p_rows] = tx4[c, p_rows] + tx4[c, u_row] * rx3b[...]
        tx4[c, end_rows] = tail_of(row, du)
        return carry

    lax.fori_loop(0, chips, carry_in, 0)

    copies4 = []
    for o in range(1, chips):
        target, device = at_chip(o)
        copies4.append(
            remote(tx4.at[target], rx4.at[chip], send4.at[o], recv4.at[o], device)
        )
        copies4[-1].start()
    rx4[chip] = tx4[chip]
    run(local_part, cuts[3], cuts[4])
    for copy in copies4:
        copy.wait_recv()

    def share(c, carry):
        ta, tb = blk[core, c, t_row], rx1[c, t_row]
        ea, eb = blk[core, c, e_rows], rx1[c, e_rows]
        pa, pb = blk[core, c, p_rows], rx1[c, p_rows]
        fc, bc, end = rx4[c, e_rows], rx4[c, p_rows], rx4[c, end_rows]
        fin[core, c, e_rows] = jnp.where(late, tb * fc + eb, fc)
        fin[core, c, p_rows] = jnp.where(late, bc, pb + tb * bc)
        fin[core, c, end_rows] = end
        tx5[c, e_rows] = jnp.where(late, fc, ta * fc + ea)
        tx5[c, p_rows] = jnp.where(late, pa + ta * bc, bc)
        tx5[c, end_rows] = end
        return carry

    lax.fori_loop(0, chips, share, 0)
    copy5 = remote(tx5, fin.at[core], core_send.at[1], core_recv.at[1], partner)
    copy5.start()
    run(local_part, cuts[4], cuts[5])
    copy5.wait_recv()
    run(finish, 0, pairs // 2)

    copy1.wait_send()
    for copy in copies2 + copies3 + copies4:
        copy.wait_send()
    copy5.wait_send()

    @pl.when(has_next)
    def _():
        ahead.wait_send()

    @pl.when(has_prev)
    def _():
        behind.wait_send()


def body(
    n,
    acceptance_gate,
    lookup_matrix,
    payload_matrix,
    fading_parameter,
    present_reward,
    emitted_cotangent,
    paper_spans,
):
    tokens, width = acceptance_gate.shape
    chips = n // GROUPS // 2
    piece = width // chips
    full = pltpu.VMEM((tokens, width), F32)
    table = pltpu.VMEM((tokens, LANES), F32)
    table2 = pltpu.VMEM((2 * tokens, LANES), F32)
    half = pltpu.VMEM((chips, BLOCK_ROWS, piece), F32)
    both = pltpu.VMEM((2, chips, BLOCK_ROWS, piece), F32)
    state = pltpu.VMEM((HALF, piece), F32)
    sems = pltpu.SemaphoreType.DMA
    grad = jax.ShapeDtypeStruct((tokens, width), BF16)
    outs = pl.pallas_call(
        functools.partial(kernel, n),
        out_shape=(grad, grad, grad, grad, jax.ShapeDtypeStruct((1, width), F32)),
        in_specs=[pl.BlockSpec(memory_space=pltpu.VMEM)] * 7,
        out_specs=[pl.BlockSpec(memory_space=pltpu.VMEM)] * 5,
        scratch_shapes=[full] * 6
        + [table2, table2, table, table, pltpu.VMEM((8, LANES), F32)]
        + [both, half, half, half, pltpu.VMEM((BLOCK_ROWS, piece), F32)]
        + [state, state, pltpu.VMEM((GROUPS - 1, 8, piece), F32)]
        + [half, half, half, both]
        + [sems((2,)), sems((2,)), sems((chips,)), sems((chips,))]
        + [sems((2,)), sems((2,)), sems((GROUPS - 1,)), sems((GROUPS - 1,))]
        + [sems((chips,)), sems((chips,))],
        compiler_params=pltpu.CompilerParams(
            collective_id=0,
            has_side_effects=True,
            vmem_limit_bytes=44 * 1024 * 1024,
        ),
    )(
        acceptance_gate,
        lookup_matrix,
        payload_matrix,
        fading_parameter,
        present_reward.reshape(1, width),
        emitted_cotangent,
        paper_spans.reshape(1, -1),
    )
    return (*outs[:4], outs[4].reshape(width))


def solution(mesh):
    row = P("seq", None)
    return jax.shard_map(
        functools.partial(body, mesh.shape["seq"]),
        mesh=mesh,
        in_specs=(row, row, row, row, P(), row, P()),
        out_specs=(row, row, row, row, P()),
        check_vma=False,
    )
```

profile of v0, /device:TPU:0, one launch (start us, length us, event | category | flops | bytes accessed | tf_op | source)
XLA Modules:
  0.0 50.1 jit_solution(6711926705683302808)
XLA Ops:
  0.6 0.0 copy-start.6
  0.6 0.6 %copy-done.6 = s32[64]{0:T(128)S(1)} copy-done((s32[64]{0:T(128)S(1)}, s32[64]{0:T(128)}, u32[]{:S(2)}) %copy-start.6) | copy-done | bytes 280
  1.3 0.0 copy-start
  1.3 1.2 %copy-done = f32[128,2048]{1,0:T(8,128)S(1)} copy-done((f32[128,2048]{1,0:T(8,128)S(1)}, f32[128,2048]{1,0:T(8,128)}, u32[]{:S(2)}) %copy-start) | copy-done | bytes 1048600
  2.5 0.0 copy-start.1
  2.5 1.0 %copy-done.1 = bf16[128,2048]{1,0:T(8,128)(2,1)S(1)} copy-done((bf16[128,2048]{1,0:T(8,128)(2,1)S(1)}, bf16[128,2048]{1,0:T(8,128)(2,1)}, u32[]{:S(2)}) %copy-start.1) | copy-done | bytes 524312
  3.6 0.0 copy-start.2
  3.6 1.0 %copy-done.2 = bf16[128,2048]{1,0:T(8,128)(2,1)S(1)} copy-done((bf16[128,2048]{1,0:T(8,128)(2,1)S(1)}, bf16[128,2048]{1,0:T(8,128)(2,1)}, u32[]{:S(2)}) %copy-start.2) | copy-done | bytes 524312
  4.6 0.0 copy-start.3
  4.6 1.0 %copy-done.3 = bf16[128,2048]{1,0:T(8,128)(2,1)S(1)} copy-done((bf16[128,2048]{1,0:T(8,128)(2,1)S(1)}, bf16[128,2048]{1,0:T(8,128)(2,1)}, u32[]{:S(2)}) %copy-start.3) | copy-done | bytes 524312
  5.6 0.0 copy-start.4
  5.6 1.0 %copy-done.4 = bf16[128,2048]{1,0:T(8,128)(2,1)S(1)} copy-done((bf16[128,2048]{1,0:T(8,128)(2,1)S(1)}, bf16[128,2048]{1,0:T(8,128)(2,1)}, u32[]{:S(2)}) %copy-start.4) | copy-done | bytes 524312
  6.7 0.0 copy-start.5
  6.7 0.7 %copy-done.5 = f32[2048]{0:T(1024)S(1)} copy-done((f32[2048]{0:T(1024)S(1)}, f32[2048]{0:T(1024)}, u32[]{:S(2)}) %copy-start.5) | copy-done | bytes 8216
  7.4 39.0 %shard_map.110 = (bf16[128,2048]{1,0:T(8,128)(2,1)S(1)}, bf16[128,2048]{1,0:T(8,128)(2,1)S(1)}, bf16[128,2048]{1,0:T(8,128)(2,1)S(1)}, bf16[128,2048]{1,0:T(8,128)(2,1)S(1)}, f32[1,2048]{1,0:T(1,128)S(1)}) custom-call(bf16[128,2048]{1,0:T(8,128)(2,1)S(1)} %copy-done.1, bf16[128,2048]{1,0:T(8,128)(2,1)S(1)} %copy-done.2, bf16[128,2048]{1,0:T(8,128)(2,1)S(1)} %copy-done.3, ...), custom_call_target="tpu_custom_call" | custom-call | tf_op jit(solution)/shard_map/pallas_call | solution.py:461
  46.4 0.8 %copy.17 = bf16[128,2048]{1,0:T(8,128)(2,1)} copy(bf16[128,2048]{1,0:T(8,128)(2,1)S(1)} %get-tuple-element.20) | data formatting | bytes 1048576
  47.2 0.8 %copy.18 = bf16[128,2048]{1,0:T(8,128)(2,1)} copy(bf16[128,2048]{1,0:T(8,128)(2,1)S(1)} %get-tuple-element.21) | data formatting | bytes 1048576
  48.0 0.8 %copy.19 = bf16[128,2048]{1,0:T(8,128)(2,1)} copy(bf16[128,2048]{1,0:T(8,128)(2,1)S(1)} %get-tuple-element.22) | data formatting | bytes 1048576
  48.8 0.8 %copy.20 = bf16[128,2048]{1,0:T(8,128)(2,1)} copy(bf16[128,2048]{1,0:T(8,128)(2,1)S(1)} %get-tuple-element.23) | data formatting | bytes 1048576
  49.5 0.6 %copy.21 = f32[2048]{0:T(1024)} copy(f32[2048]{0:T(1024)S(1)} %bitcast.4) | data formatting | bytes 16384
Async XLA Ops:
  0.6 0.7 %copy-start.6 = (s32[64]{0:T(128)S(1)}, s32[64]{0:T(128)}, u32[]{:S(2)}) copy-start(s32[64]{0:T(128)} %param.13) | copy-start | bytes 772
  1.3 1.2 %copy-start = (f32[128,2048]{1,0:T(8,128)S(1)}, f32[128,2048]{1,0:T(8,128)}, u32[]{:S(2)}) copy-start(f32[128,2048]{1,0:T(8,128)} %x_ref.1) | copy-start | bytes 3145732
  2.5 1.0 %copy-start.1 = (bf16[128,2048]{1,0:T(8,128)(2,1)S(1)}, bf16[128,2048]{1,0:T(8,128)(2,1)}, u32[]{:S(2)}) copy-start(bf16[128,2048]{1,0:T(8,128)(2,1)} %r_ref.1) | copy-start | bytes 1572868
  3.6 1.0 %copy-start.2 = (bf16[128,2048]{1,0:T(8,128)(2,1)S(1)}, bf16[128,2048]{1,0:T(8,128)(2,1)}, u32[]{:S(2)}) copy-start(bf16[128,2048]{1,0:T(8,128)(2,1)} %k_ref.1) | copy-start | bytes 1572868
  4.6 1.0 %copy-start.3 = (bf16[128,2048]{1,0:T(8,128)(2,1)S(1)}, bf16[128,2048]{1,0:T(8,128)(2,1)}, u32[]{:S(2)}) copy-start(bf16[128,2048]{1,0:T(8,128)(2,1)} %v_ref.1) | copy-start | bytes 1572868
  5.6 1.0 %copy-start.4 = (bf16[128,2048]{1,0:T(8,128)(2,1)S(1)}, bf16[128,2048]{1,0:T(8,128)(2,1)}, u32[]{:S(2)}) copy-start(bf16[128,2048]{1,0:T(8,128)(2,1)} %dy_ref.1) | copy-start | bytes 1572868
  6.7 0.7 %copy-start.5 = (f32[2048]{0:T(1024)S(1)}, f32[2048]{0:T(1024)}, u32[]{:S(2)}) copy-start(f32[2048]{0:T(1024)} %param.11) | copy-start | bytes 24580
where the time goes:
time: 50.9 us; the launch traced here: 50.1 us
  Pallas kernels  39 us (77%)
  local copies, waits for them, and re-layouts  10.5 us (21%)
  between operations  0.66 us (1%)
    pallas_call x1, Pallas kernels, body(): pl.pallas_call(functools.partial(kernel, n), out_shape=(grad, grad, grad,...  39 us
    unnamed x19, local copies, waits for them, and re-layouts  10.5 us

commit v1 on v0

--- a/solution.py
+++ b/solution.py
@@ -49,6 +49,18 @@
 
 def kernel(
     n,
+    r_hbm,
+    k_hbm,
+    v_hbm,
+    x_hbm,
+    u_hbm,
+    dy_hbm,
+    spans_hbm,
+    dr_ref,
+    dk_ref,
+    dv_ref,
+    dx_ref,
+    du_ref,
     r_ref,
     k_ref,
     v_ref,
@@ -56,11 +68,6 @@
     u_ref,
     dy_ref,
     spans_ref,
-    dr_ref,
-    dk_ref,
-    dv_ref,
-    dx_ref,
-    du_ref,
     lw_s,
     cum_s,
     dyv_s,
@@ -84,6 +91,8 @@
     rx4,
     tx5,
     fin,
+    in_sem,
+    small_sem,
     core_send,
     core_recv,
     send2,
@@ -120,6 +129,33 @@
     for friend in friends:
         pl.semaphore_signal(barrier, inc=1, device_id=(friend,), device_id_type=MESH)
 
+    load_spans = pltpu.make_async_copy(spans_hbm, spans_ref, small_sem.at[0])
+    load_u = pltpu.make_async_copy(u_hbm, u_ref, small_sem.at[1])
+    load_spans.start()
+    load_u.start()
+    large = (
+        (x_hbm, x_ref),
+        (k_hbm, k_ref),
+        (r_hbm, r_ref),
+        (v_hbm, v_ref),
+        (dy_hbm, dy_ref),
+    )
+    loads = []
+    for o in range(1, chips + 1):
+        target = lax.rem(chip + o, chips)
+        cols = pl.ds(pl.multiple_of(target * piece, LANES), piece)
+        loads.append(
+            [
+                pltpu.make_async_copy(
+                    src.at[:, cols], dst.at[:, cols], in_sem.at[i * chips + o - 1]
+                )
+                for i, (src, dst) in enumerate(large)
+            ]
+        )
+        for load in loads[-1]:
+            load.start()
+
+    load_spans.wait()
     docs = spans_ref.shape[1]
     spans_row = spans_ref[...].astype(F32)
     one = lax.broadcasted_iota(jnp.int32, (docs, docs), 0)
@@ -252,16 +288,22 @@
         dx_ref[:, cols] = (rev * lw).astype(BF16)
         du_ref[:, cols] = fin[0, slot, 2 * HALF + 1 : 2 * HALF + 2, sub]
 
-    def run(part, low, high):
+    per = piece // LANES
+
+    def run(part, low, count):
+        if count % 2:
+            for i in range(count):
+                part(low + i)
+            return
+
         def step(i, carry):
-            part(2 * i)
-            part(2 * i + 1)
+            part(low + 2 * i)
+            part(low + 2 * i + 1)
             return carry
 
-        lax.fori_loop(low, high, step, 0)
-
-    cuts = [pairs * c // 16 for c in (0, 1, 4, 5, 7, 8)]
-    run(summarise, 0, pairs // 2)
+        lax.fori_loop(0, count // 2, step, 0)
+
+    cuts = [pairs * c // 16 for c in (0, 2, 6, 10, 14, 16)]
 
     def remote(src, dst, send, recv, device):
         return pltpu.make_async_remote_copy(
@@ -273,12 +315,6 @@
             device_id_type=MESH,
         )
 
-    pl.semaphore_wait(barrier, len(friends))
-
-    copy1 = remote(blk.at[1 - core], rx1, core_send.at[0], core_recv.at[0], partner)
-    copy1.start()
-    run(local_part, cuts[0], cuts[1])
-    copy1.wait_recv()
     late = core == 1
     e_rows, p_rows = slice(0, HALF), slice(HALF, 2 * HALF)
     t_row, u_row = slice(2 * HALF, 2 * HALF + 1), slice(2 * HALF + 1, 2 * HALF + 2)
@@ -287,26 +323,50 @@
     def tail_of(t, u):
         return rows(t, u, jnp.zeros((6, piece), F32))
 
-    def combine(c, carry):
+    def combine(c, out):
         ta, tb = blk[core, c, t_row], rx1[c, t_row]
         ea, eb = blk[core, c, e_rows], rx1[c, e_rows]
         pa, pb = blk[core, c, p_rows], rx1[c, p_rows]
-        tx2[c, e_rows] = jnp.where(late, ta * eb + ea, tb * ea + eb)
-        tx2[c, p_rows] = jnp.where(late, pb + tb * pa, pa + ta * pb)
-        tx2[c, end_rows] = tail_of(ta * tb, blk[core, c, u_row] + rx1[c, u_row])
-        return carry
-
-    lax.fori_loop(0, chips, combine, 0)
-
-    copies2 = []
-    for o in range(1, chips):
+        out[c, e_rows] = jnp.where(late, ta * eb + ea, tb * ea + eb)
+        out[c, p_rows] = jnp.where(late, pb + tb * pa, pa + ta * pb)
+        out[c, end_rows] = tail_of(ta * tb, blk[core, c, u_row] + rx1[c, u_row])
+
+    copies1, copies2 = [], []
+
+    def pass_on(o):
+        copies1[o - 1].wait_recv()
         target, device = at_chip(o)
+        if o == chips:
+            combine(chip, rx2)
+            return
+        combine(target, tx2)
         copies2.append(
             remote(tx2.at[target], rx2.at[chip], send2.at[o], recv2.at[o], device)
         )
         copies2[-1].start()
-    rx2[chip] = tx2[chip]
-    run(local_part, cuts[1], cuts[2])
+
+    for o in range(1, chips + 1):
+        target, _ = at_chip(o)
+        for load in loads[o - 1]:
+            load.wait()
+        run(summarise, target * per, per)
+        if o == 1:
+            pl.semaphore_wait(barrier, len(friends))
+        copies1.append(
+            remote(
+                blk.at[1 - core, target],
+                rx1.at[target],
+                core_send.at[o - 1],
+                core_recv.at[o - 1],
+                partner,
+            )
+        )
+        copies1[-1].start()
+        if o > 1:
+            pass_on(o - 1)
+    run(local_part, cuts[0], cuts[1] - cuts[0])
+    pass_on(chips)
+    run(local_part, cuts[1], cuts[2] - cuts[1])
     for copy in copies2:
         copy.wait_recv()
 
@@ -359,7 +419,7 @@
             )
         )
         copies3[-1].start()
-    run(local_part, cuts[2], cuts[3])
+    run(local_part, cuts[2], cuts[3] - cuts[2])
 
     @pl.when(has_prev)
     def _():
@@ -399,34 +459,47 @@
         )
         copies4[-1].start()
     rx4[chip] = tx4[chip]
-    run(local_part, cuts[3], cuts[4])
-    for copy in copies4:
-        copy.wait_recv()
-
-    def share(c, carry):
+
+    copies5 = []
+
+    def share(o):
+        c = lax.rem(chip - o + chips, chips)
+        if o:
+            copies4[o - 1].wait_recv()
         ta, tb = blk[core, c, t_row], rx1[c, t_row]
         ea, eb = blk[core, c, e_rows], rx1[c, e_rows]
         pa, pb = blk[core, c, p_rows], rx1[c, p_rows]
         fc, bc, end = rx4[c, e_rows], rx4[c, p_rows], rx4[c, end_rows]
+        tx5[c, e_rows] = jnp.where(late, fc, ta * fc + ea)
+        tx5[c, p_rows] = jnp.where(late, pa + ta * bc, bc)
+        tx5[c, end_rows] = end
+        copies5.append(
+            remote(
+                tx5.at[c],
+                fin.at[core, c],
+                core_send.at[chips + o],
+                core_recv.at[chips + o],
+                partner,
+            )
+        )
+        copies5[-1].start()
         fin[core, c, e_rows] = jnp.where(late, tb * fc + eb, fc)
         fin[core, c, p_rows] = jnp.where(late, bc, pb + tb * bc)
         fin[core, c, end_rows] = end
-        tx5[c, e_rows] = jnp.where(late, fc, ta * fc + ea)
-        tx5[c, p_rows] = jnp.where(late, pa + ta * bc, bc)
-        tx5[c, end_rows] = end
-        return carry
-
-    lax.fori_loop(0, chips, share, 0)
-    copy5 = remote(tx5, fin.at[core], core_send.at[1], core_recv.at[1], partner)
-    copy5.start()
-    run(local_part, cuts[4], cuts[5])
-    copy5.wait_recv()
-    run(finish, 0, pairs // 2)
-
-    copy1.wait_send()
-    for copy in copies2 + copies3 + copies4:
+
+    share(0)
+    run(local_part, cuts[3], cuts[4] - cuts[3])
+    share(1)
+    run(local_part, cuts[4], cuts[5] - cuts[4])
+    load_u.wait()
+    for o in range(chips):
+        if o + 2 < chips:
+            share(o + 2)
+        copies5[o].wait_recv()
+        run(finish, lax.rem(chip - o + chips, chips) * per, per)
+
+    for copy in copies1 + copies2 + copies3 + copies4 + copies5:
         copy.wait_send()
-    copy5.wait_send()
 
     @pl.when(has_next)
     def _():
@@ -451,6 +524,7 @@
     chips = n // GROUPS // 2
     piece = width // chips
     full = pltpu.VMEM((tokens, width), F32)
+    given = pltpu.VMEM((tokens, width), BF16)
     table = pltpu.VMEM((tokens, LANES), F32)
     table2 = pltpu.VMEM((2 * tokens, LANES), F32)
     half = pltpu.VMEM((chips, BLOCK_ROWS, piece), F32)
@@ -461,14 +535,18 @@
     outs = pl.pallas_call(
         functools.partial(kernel, n),
         out_shape=(grad, grad, grad, grad, jax.ShapeDtypeStruct((1, width), F32)),
-        in_specs=[pl.BlockSpec(memory_space=pltpu.VMEM)] * 7,
+        in_specs=[pl.BlockSpec(memory_space=pltpu.HBM)] * 7,
         out_specs=[pl.BlockSpec(memory_space=pltpu.VMEM)] * 5,
-        scratch_shapes=[full] * 6
+        scratch_shapes=[given, given, given, full]
+        + [pltpu.VMEM((1, width), F32), given]
+        + [pltpu.VMEM((1, paper_spans.shape[0]), jnp.int32)]
+        + [full] * 6
         + [table2, table2, table, table, pltpu.VMEM((8, LANES), F32)]
         + [both, half, half, half, pltpu.VMEM((BLOCK_ROWS, piece), F32)]
         + [state, state, pltpu.VMEM((GROUPS - 1, 8, piece), F32)]
         + [half, half, half, both]
-        + [sems((2,)), sems((2,)), sems((chips,)), sems((chips,))]
+        + [sems((5 * chips,)), sems((2,)), sems((2 * chips,)), sems((2 * chips,))]
+        + [sems((chips,)), sems((chips,))]
         + [sems((2,)), sems((2,)), sems((GROUPS - 1,)), sems((GROUPS - 1,))]
         + [sems((chips,)), sems((chips,))],
         compiler_params=pltpu.CompilerParams(

time: 50.9 us -> 45.1 us (0.89)
  Pallas kernels: 39 us -> 33.5 us
    pallas_call x1, Pallas kernels: 39 us -> 33.5 us  [body(): pl.pallas_call(functools.partial(kernel, n), out_shape=(grad, grad, grad,...]
where the time goes in v1:
time: 45.1 us; the launch traced here: 44.7 us
  Pallas kernels  33.5 us (74%)
  local copies, waits for them, and re-layouts  10.5 us (23%)
  between operations  0.66 us (1%)
    pallas_call x1, Pallas kernels, body(): pl.pallas_call(functools.partial(kernel, n), out_shape=(grad, grad, grad,...  33.5 us
    unnamed x19, local copies, waits for them, and re-layouts  10.5 us

profile of v1, /device:TPU:0, one launch (start us, length us, event | category | flops | bytes accessed | tf_op | source)
XLA Modules:
  0.0 44.7 jit_solution(12493993199179363270)
XLA Ops:
  0.6 0.0 copy-start.6
  0.6 0.6 %copy-done.6 = s32[64]{0:T(128)S(1)} copy-done((s32[64]{0:T(128)S(1)}, s32[64]{0:T(128)}, u32[]{:S(2)}) %copy-start.6) | copy-done | bytes 280
  1.3 0.0 copy-start
  1.3 1.2 %copy-done = f32[128,2048]{1,0:T(8,128)S(1)} copy-done((f32[128,2048]{1,0:T(8,128)S(1)}, f32[128,2048]{1,0:T(8,128)}, u32[]{:S(2)}) %copy-start) | copy-done | bytes 1048600
  2.5 0.0 copy-start.1
  2.5 1.0 %copy-done.1 = bf16[128,2048]{1,0:T(8,128)(2,1)S(1)} copy-done((bf16[128,2048]{1,0:T(8,128)(2,1)S(1)}, bf16[128,2048]{1,0:T(8,128)(2,1)}, u32[]{:S(2)}) %copy-start.1) | copy-done | bytes 524312
  3.6 0.0 copy-start.2
  3.6 1.0 %copy-done.2 = bf16[128,2048]{1,0:T(8,128)(2,1)S(1)} copy-done((bf16[128,2048]{1,0:T(8,128)(2,1)S(1)}, bf16[128,2048]{1,0:T(8,128)(2,1)}, u32[]{:S(2)}) %copy-start.2) | copy-done | bytes 524312
  4.6 0.0 copy-start.3
  4.6 1.0 %copy-done.3 = bf16[128,2048]{1,0:T(8,128)(2,1)S(1)} copy-done((bf16[128,2048]{1,0:T(8,128)(2,1)S(1)}, bf16[128,2048]{1,0:T(8,128)(2,1)}, u32[]{:S(2)}) %copy-start.3) | copy-done | bytes 524312
  5.6 0.0 copy-start.4
  5.6 1.0 %copy-done.4 = bf16[128,2048]{1,0:T(8,128)(2,1)S(1)} copy-done((bf16[128,2048]{1,0:T(8,128)(2,1)S(1)}, bf16[128,2048]{1,0:T(8,128)(2,1)}, u32[]{:S(2)}) %copy-start.4) | copy-done | bytes 524312
  6.7 0.0 copy-start.5
  6.7 0.7 %copy-done.5 = f32[2048]{0:T(1024)S(1)} copy-done((f32[2048]{0:T(1024)S(1)}, f32[2048]{0:T(1024)}, u32[]{:S(2)}) %copy-start.5) | copy-done | bytes 8216
  7.4 33.5 %shard_map.110 = (bf16[128,2048]{1,0:T(8,128)(2,1)S(1)}, bf16[128,2048]{1,0:T(8,128)(2,1)S(1)}, bf16[128,2048]{1,0:T(8,128)(2,1)S(1)}, bf16[128,2048]{1,0:T(8,128)(2,1)S(1)}, f32[1,2048]{1,0:T(1,128)S(1)}) custom-call(bf16[128,2048]{1,0:T(8,128)(2,1)S(1)} %copy-done.1, bf16[128,2048]{1,0:T(8,128)(2,1)S(1)} %copy-done.2, bf16[128,2048]{1,0:T(8,128)(2,1)S(1)} %copy-done.3, ...), custom_call_target="tpu_custom_call" | custom-call | tf_op jit(solution)/shard_map/pallas_call | solution.py:535
  40.9 0.8 %copy.17 = bf16[128,2048]{1,0:T(8,128)(2,1)} copy(bf16[128,2048]{1,0:T(8,128)(2,1)S(1)} %get-tuple-element.20) | data formatting | bytes 1048576
  41.7 0.8 %copy.18 = bf16[128,2048]{1,0:T(8,128)(2,1)} copy(bf16[128,2048]{1,0:T(8,128)(2,1)S(1)} %get-tuple-element.21) | data formatting | bytes 1048576
  42.5 0.8 %copy.19 = bf16[128,2048]{1,0:T(8,128)(2,1)} copy(bf16[128,2048]{1,0:T(8,128)(2,1)S(1)} %get-tuple-element.22) | data formatting | bytes 1048576
  43.3 0.8 %copy.20 = bf16[128,2048]{1,0:T(8,128)(2,1)} copy(bf16[128,2048]{1,0:T(8,128)(2,1)S(1)} %get-tuple-element.23) | data formatting | bytes 1048576
  44.1 0.6 %copy.21 = f32[2048]{0:T(1024)} copy(f32[2048]{0:T(1024)S(1)} %bitcast.4) | data formatting | bytes 16384
Async XLA Ops:
  0.6 0.7 %copy-start.6 = (s32[64]{0:T(128)S(1)}, s32[64]{0:T(128)}, u32[]{:S(2)}) copy-start(s32[64]{0:T(128)} %param.13) | copy-start | bytes 772
  1.3 1.2 %copy-start = (f32[128,2048]{1,0:T(8,128)S(1)}, f32[128,2048]{1,0:T(8,128)}, u32[]{:S(2)}) copy-start(f32[128,2048]{1,0:T(8,128)} %x_hbm.1) | copy-start | bytes 3145732
  2.5 1.0 %copy-start.1 = (bf16[128,2048]{1,0:T(8,128)(2,1)S(1)}, bf16[128,2048]{1,0:T(8,128)(2,1)}, u32[]{:S(2)}) copy-start(bf16[128,2048]{1,0:T(8,128)(2,1)} %r_hbm.1) | copy-start | bytes 1572868
  3.6 1.0 %copy-start.2 = (bf16[128,2048]{1,0:T(8,128)(2,1)S(1)}, bf16[128,2048]{1,0:T(8,128)(2,1)}, u32[]{:S(2)}) copy-start(bf16[128,2048]{1,0:T(8,128)(2,1)} %k_hbm.1) | copy-start | bytes 1572868
  4.6 1.0 %copy-start.3 = (bf16[128,2048]{1,0:T(8,128)(2,1)S(1)}, bf16[128,2048]{1,0:T(8,128)(2,1)}, u32[]{:S(2)}) copy-start(bf16[128,2048]{1,0:T(8,128)(2,1)} %v_hbm.1) | copy-start | bytes 1572868
  5.6 1.0 %copy-start.4 = (bf16[128,2048]{1,0:T(8,128)(2,1)S(1)}, bf16[128,2048]{1,0:T(8,128)(2,1)}, u32[]{:S(2)}) copy-start(bf16[128,2048]{1,0:T(8,128)(2,1)} %dy_hbm.1) | copy-start | bytes 1572868
  6.7 0.7 %copy-start.5 = (f32[2048]{0:T(1024)S(1)}, f32[2048]{0:T(1024)}, u32[]{:S(2)}) copy-start(f32[2048]{0:T(1024)} %param.11) | copy-start | bytes 24580

commit v2 on v1

--- a/solution.py
+++ b/solution.py
@@ -12,6 +12,7 @@
 HALF = 32
 BLOCK_ROWS = 72
 GROUPS = 4
+VMEM_LIMIT = 62 * 1024 * 1024
 MESH = pl.DeviceIdType.MESH
 F32 = jnp.float32
 BF16 = jnp.bfloat16
@@ -56,6 +57,11 @@
     u_hbm,
     dy_hbm,
     spans_hbm,
+    dr_hbm,
+    dk_hbm,
+    dv_hbm,
+    dx_hbm,
+    du_hbm,
     dr_ref,
     dk_ref,
     dv_ref,
@@ -92,6 +98,7 @@
     tx5,
     fin,
     in_sem,
+    out_sem,
     small_sem,
     core_send,
     core_recv,
@@ -492,11 +499,30 @@
     share(1)
     run(local_part, cuts[4], cuts[5] - cuts[4])
     load_u.wait()
+    results = (
+        (dr_ref, dr_hbm),
+        (dk_ref, dk_hbm),
+        (dv_ref, dv_hbm),
+        (dx_ref, dx_hbm),
+        (du_ref, du_hbm),
+    )
+    stores = []
     for o in range(chips):
         if o + 2 < chips:
             share(o + 2)
         copies5[o].wait_recv()
-        run(finish, lax.rem(chip - o + chips, chips) * per, per)
+        target = lax.rem(chip - o + chips, chips)
+        run(finish, target * per, per)
+        cols = pl.ds(pl.multiple_of(target * piece, LANES), piece)
+        for i, (src, dst) in enumerate(results):
+            stores.append(
+                pltpu.make_async_copy(
+                    src.at[:, cols], dst.at[:, cols], out_sem.at[i * chips + o]
+                )
+            )
+            stores[-1].start()
+    for store in stores:
+        store.wait()
 
     for copy in copies1 + copies2 + copies3 + copies4 + copies5:
         copy.wait_send()
@@ -508,6 +534,18 @@
     @pl.when(has_prev)
     def _():
         behind.wait_send()
+
+
+def hand_over(*refs):
+    sem = refs[-1]
+    count = len(refs) // 2
+    copies = [
+        pltpu.make_async_copy(refs[i], refs[count + i], sem.at[i]) for i in range(count)
+    ]
+    for copy in copies:
+        copy.start()
+    for copy in copies:
+        copy.wait()
 
 
 def body(
@@ -536,8 +574,10 @@
         functools.partial(kernel, n),
         out_shape=(grad, grad, grad, grad, jax.ShapeDtypeStruct((1, width), F32)),
         in_specs=[pl.BlockSpec(memory_space=pltpu.HBM)] * 7,
-        out_specs=[pl.BlockSpec(memory_space=pltpu.VMEM)] * 5,
-        scratch_shapes=[given, given, given, full]
+        out_specs=[pl.BlockSpec(memory_space=pltpu.HBM)] * 5,
+        scratch_shapes=[given] * 4
+        + [pltpu.VMEM((1, width), F32)]
+        + [given, given, given, full]
         + [pltpu.VMEM((1, width), F32), given]
         + [pltpu.VMEM((1, paper_spans.shape[0]), jnp.int32)]
         + [full] * 6
@@ -545,14 +585,14 @@
         + [both, half, half, half, pltpu.VMEM((BLOCK_ROWS, piece), F32)]
         + [state, state, pltpu.VMEM((GROUPS - 1, 8, piece), F32)]
         + [half, half, half, both]
-        + [sems((5 * chips,)), sems((2,)), sems((2 * chips,)), sems((2 * chips,))]
+        + [sems((5 * chips,)), sems((5 * chips,)), sems((2,)), sems((2 * chips,)), sems((2 * chips,))]
         + [sems((chips,)), sems((chips,))]
         + [sems((2,)), sems((2,)), sems((GROUPS - 1,)), sems((GROUPS - 1,))]
         + [sems((chips,)), sems((chips,))],
         compiler_params=pltpu.CompilerParams(
             collective_id=0,
             has_side_effects=True,
-            vmem_limit_bytes=44 * 1024 * 1024,
+            vmem_limit_bytes=VMEM_LIMIT,
         ),
     )(
         acceptance_gate,
@@ -563,6 +603,14 @@
         emitted_cotangent,
         paper_spans.reshape(1, -1),
     )
+    outs = pl.pallas_call(
+        hand_over,
+        out_shape=[jax.ShapeDtypeStruct(out.shape, out.dtype) for out in outs],
+        in_specs=[pl.BlockSpec(memory_space=pltpu.HBM)] * 5,
+        out_specs=[pl.BlockSpec(memory_space=pltpu.HBM)] * 5,
+        scratch_shapes=[sems((5,))],
+        compiler_params=pltpu.CompilerParams(vmem_limit_bytes=VMEM_LIMIT),
+    )(*outs)
     return (*outs[:4], outs[4].reshape(width))
 
 

time: 45.1 us -> 101 us (2.24)
  Pallas kernels: 33.5 us -> 100 us
  local copies, waits for them, and re-layouts: 10.5 us -> 0 us
    pallas_call x0 -> x1, Pallas kernels: none -> 64.9 us  [body(): pl.pallas_call(hand_over, out_shape=[jax.ShapeDtypeStruct(out.shape, out....]
    unnamed x19 -> x0, local copies, waits for them, and re-layouts: 10.5 us -> none
    pallas_call x1, Pallas kernels: 33.5 us -> 35.5 us  [body(): pl.pallas_call(functools.partial(kernel, n), out_shape=(grad, grad, grad,...]
where the time goes in v2:
time: 101 us
  Pallas kernels  100 us (99%)
    pallas_call x1, Pallas kernels, body(): pl.pallas_call(hand_over, out_shape=[jax.ShapeDtypeStruct(out.shape, out....  64.9 us
    pallas_call x1, Pallas kernels, body(): pl.pallas_call(functools.partial(kernel, n), out_shape=(grad, grad, grad,...  35.5 us

profile of v2, /device:TPU:0, one launch (start us, length us, event | category | flops | bytes accessed | tf_op | source)
XLA Modules:
  0.0 101.0 jit_solution(9699191177988858875)
XLA Ops:
  0.6 35.5 %shard_map.110 = (bf16[128,2048]{1,0:T(8,128)(2,1)}, bf16[128,2048]{1,0:T(8,128)(2,1)}, bf16[128,2048]{1,0:T(8,128)(2,1)}, bf16[128,2048]{1,0:T(8,128)(2,1)}, f32[1,2048]{1,0:T(1,128)}) custom-call(bf16[128,2048]{1,0:T(8,128)(2,1)} %r_hbm.1, bf16[128,2048]{1,0:T(8,128)(2,1)} %k_hbm.1, bf16[128,2048]{1,0:T(8,128)(2,1)} %v_hbm.1, f32[128,2048]{1,0:T(8,128)} %x_hbm.1, ...), custom_call_target="tpu_custom_call" | custom-call | tf_op jit(solution)/shard_map/pallas_call | solution.py:573
  36.1 64.9 %shard_map.111 = (bf16[128,2048]{1,0:T(8,128)(2,1)}, bf16[128,2048]{1,0:T(8,128)(2,1)}, bf16[128,2048]{1,0:T(8,128)(2,1)}, bf16[128,2048]{1,0:T(8,128)(2,1)}, f32[1,2048]{1,0:T(1,128)}) custom-call(bf16[128,2048]{1,0:T(8,128)(2,1)} %get-tuple-element.15.refs_0_, bf16[128,2048]{1,0:T(8,128)(2,1)} %get-tuple-element.16.refs_1_, ...), custom_call_target="tpu_custom_call" | custom-call | tf_op jit(solution)/shard_map/pallas_call | solution.py:606

commit v3 on v2

--- a/solution.py
+++ b/solution.py
@@ -198,12 +198,11 @@
     lower = jnp.where(first >= second, 1.0, 0.0).astype(BF16)
     upper = jnp.where(first <= second, 1.0, 0.0).astype(BF16)
     lower3 = lanes(lower, lower, lower)
-    upper3 = lanes(upper, upper, upper)
+    upper2 = lanes(upper, upper)
     head_i = lax.broadcasted_iota(jnp.int32, (LANES, LANES), 0) // HS
     head_j = lax.broadcasted_iota(jnp.int32, (LANES, LANES), 1) // HS
     ones = jnp.where(head_i == head_j, 1.0, 0.0).astype(BF16)
     ones2 = rows(ones, ones)
-    ones3 = rows(ones, ones, ones)
 
     def stacked(x):
         return rows(x * mask_a, x * mask_b)
@@ -277,7 +276,7 @@
         ending = k * fade
         eh, el = split2(ending)
         eb, enc = jnp.exp(cum - lw), jnp.exp(-cum)
-        bonus = dot(lanes(*split3(r * u * k)), ones3)
+        bonus = dot(lanes(*split2(r * u * k)), ones2)
         dkk = dkk_s[:, cols]
         dv = dvv_s[:, cols] + dot_nt(lanes(eh, el, eh), lanes(gh, gh, gl))
         dv = dv + bonus * dy.astype(F32)
@@ -291,24 +290,22 @@
         tail = jnp.sum(ee, axis=0, keepdims=True)
         tail = tail + through * jnp.sum(s * g, axis=0, keepdims=True)
         total = db - dkk * (k * enc) - ee
-        rev = dot(upper3, rows(*split3(total))) + tail - db
+        rev = dot(upper2, rows(*split2(total))) + tail - db
         dx_ref[:, cols] = (rev * lw).astype(BF16)
         du_ref[:, cols] = fin[0, slot, 2 * HALF + 1 : 2 * HALF + 2, sub]
 
     per = piece // LANES
 
-    def run(part, low, count):
-        if count % 2:
-            for i in range(count):
-                part(low + i)
-            return
+    def run(part, low, count, width=2):
+        if count % width:
+            width = 1
 
         def step(i, carry):
-            part(low + 2 * i)
-            part(low + 2 * i + 1)
+            for j in range(width):
+                part(low + width * i + j)
             return carry
 
-        lax.fori_loop(0, count // 2, step, 0)
+        lax.fori_loop(0, count // width, step, 0)
 
     cuts = [pairs * c // 16 for c in (0, 2, 6, 10, 14, 16)]
 
@@ -356,7 +353,7 @@
         target, _ = at_chip(o)
         for load in loads[o - 1]:
             load.wait()
-        run(summarise, target * per, per)
+        run(summarise, target * per, per, 4)
         if o == 1:
             pl.semaphore_wait(barrier, len(friends))
         copies1.append(
@@ -512,7 +509,7 @@
             share(o + 2)
         copies5[o].wait_recv()
         target = lax.rem(chip - o + chips, chips)
-        run(finish, target * per, per)
+        run(finish, target * per, per, 4)
         cols = pl.ds(pl.multiple_of(target * piece, LANES), piece)
         for i, (src, dst) in enumerate(results):
             stores.append(
@@ -537,15 +534,22 @@
 
 
 def hand_over(*refs):
+    count = len(refs) // 3
     sem = refs[-1]
-    count = len(refs) // 2
     copies = [
-        pltpu.make_async_copy(refs[i], refs[count + i], sem.at[i]) for i in range(count)
+        [
+            pltpu.make_async_copy(refs[i], refs[2 * count + i], sem.at[i]),
+            pltpu.make_async_copy(refs[2 * count + i], refs[count + i], sem.at[count + i]),
+        ]
+        for i in range(count)
     ]
-    for copy in copies:
-        copy.start()
-    for copy in copies:
-        copy.wait()
+    for load, _ in copies:
+        load.start()
+    for load, store in copies:
+        load.wait()
+        store.start()
+    for _, store in copies:
+        store.wait()
 
 
 def body(
@@ -608,7 +612,7 @@
         out_shape=[jax.ShapeDtypeStruct(out.shape, out.dtype) for out in outs],
         in_specs=[pl.BlockSpec(memory_space=pltpu.HBM)] * 5,
         out_specs=[pl.BlockSpec(memory_space=pltpu.HBM)] * 5,
-        scratch_shapes=[sems((5,))],
+        scratch_shapes=[pltpu.VMEM(out.shape, out.dtype) for out in outs] + [sems((10,))],
         compiler_params=pltpu.CompilerParams(vmem_limit_bytes=VMEM_LIMIT),
     )(*outs)
     return (*outs[:4], outs[4].reshape(width))

time: 101 us -> 37.6 us (0.37)
  Pallas kernels: 100 us -> 36.9 us
    pallas_call x1, Pallas kernels: 64.9 us -> 2.44 us  [body(): pl.pallas_call(hand_over, out_shape=[jax.ShapeDtypeStruct(out.shape, out....]
    pallas_call x1, Pallas kernels: 35.5 us -> 34.4 us  [body(): pl.pallas_call(functools.partial(kernel, n), out_shape=(grad, grad, grad,...]
where the time goes in v3:
time: 37.6 us; the launch traced here: 37.5 us
  Pallas kernels  36.9 us (98%)
  between operations  0.64 us (2%)
    pallas_call x1, Pallas kernels, body(): pl.pallas_call(functools.partial(kernel, n), out_shape=(grad, grad, grad,...  34.4 us
    pallas_call x1, Pallas kernels, body(): pl.pallas_call(hand_over, out_shape=[jax.ShapeDtypeStruct(out.shape, out....  2.44 us

profile of v3, /device:TPU:0, one launch (start us, length us, event | category | flops | bytes accessed | tf_op | source)
XLA Modules:
  0.0 37.5 jit_solution(9888306757535128720)
XLA Ops:
  0.6 34.4 %shard_map.110 = (bf16[128,2048]{1,0:T(8,128)(2,1)}, bf16[128,2048]{1,0:T(8,128)(2,1)}, bf16[128,2048]{1,0:T(8,128)(2,1)}, bf16[128,2048]{1,0:T(8,128)(2,1)}, f32[1,2048]{1,0:T(1,128)}) custom-call(bf16[128,2048]{1,0:T(8,128)(2,1)} %r_hbm.1, bf16[128,2048]{1,0:T(8,128)(2,1)} %k_hbm.1, bf16[128,2048]{1,0:T(8,128)(2,1)} %v_hbm.1, f32[128,2048]{1,0:T(8,128)} %x_hbm.1, ...), custom_call_target="tpu_custom_call" | custom-call | tf_op jit(solution)/shard_map/pallas_call | solution.py:577
  35.1 2.4 %shard_map.111 = (bf16[128,2048]{1,0:T(8,128)(2,1)}, bf16[128,2048]{1,0:T(8,128)(2,1)}, bf16[128,2048]{1,0:T(8,128)(2,1)}, bf16[128,2048]{1,0:T(8,128)(2,1)}, f32[1,2048]{1,0:T(1,128)}) custom-call(bf16[128,2048]{1,0:T(8,128)(2,1)} %get-tuple-element.15.refs_0_, bf16[128,2048]{1,0:T(8,128)(2,1)} %get-tuple-element.16.refs_1_, ...), custom_call_target="tpu_custom_call" | custom-call | tf_op jit(solution)/shard_map/pallas_call | solution.py:610

commit v4 on v3

--- a/solution.py
+++ b/solution.py
@@ -296,9 +296,9 @@
 
     per = piece // LANES
 
-    def run(part, low, count, width=2):
-        if count % width:
-            width = 1
+    def run(part, low, count, width=4):
+        while count % width:
+            width //= 2
 
         def step(i, carry):
             for j in range(width):

time: 37.6 us -> 37.8 us (level)
  no operation moved by 1% of the time
where the time goes in v4:
time: 37.8 us; the launch traced here: 37.7 us
  Pallas kernels  36.9 us (98%)
  between operations  0.8 us (2%)
    pallas_call x1, Pallas kernels, body(): pl.pallas_call(functools.partial(kernel, n), out_shape=(grad, grad, grad,...  34.4 us
    pallas_call x1, Pallas kernels, body(): pl.pallas_call(hand_over, out_shape=[jax.ShapeDtypeStruct(out.shape, out....  2.44 us

profile of v4, /device:TPU:0, one launch (start us, length us, event | category | flops | bytes accessed | tf_op | source)
XLA Modules:
  0.0 37.7 jit_solution(10630160293516296236)
XLA Ops:
  0.6 34.4 %shard_map.110 = (bf16[128,2048]{1,0:T(8,128)(2,1)}, bf16[128,2048]{1,0:T(8,128)(2,1)}, bf16[128,2048]{1,0:T(8,128)(2,1)}, bf16[128,2048]{1,0:T(8,128)(2,1)}, f32[1,2048]{1,0:T(1,128)}) custom-call(bf16[128,2048]{1,0:T(8,128)(2,1)} %r_hbm.1, bf16[128,2048]{1,0:T(8,128)(2,1)} %k_hbm.1, bf16[128,2048]{1,0:T(8,128)(2,1)} %v_hbm.1, f32[128,2048]{1,0:T(8,128)} %x_hbm.1, ...), custom_call_target="tpu_custom_call" | custom-call | tf_op jit(solution)/shard_map/pallas_call | solution.py:577
  35.1 2.4 %shard_map.111 = (bf16[128,2048]{1,0:T(8,128)(2,1)}, bf16[128,2048]{1,0:T(8,128)(2,1)}, bf16[128,2048]{1,0:T(8,128)(2,1)}, bf16[128,2048]{1,0:T(8,128)(2,1)}, f32[1,2048]{1,0:T(1,128)}) custom-call(bf16[128,2048]{1,0:T(8,128)(2,1)} %get-tuple-element.15.refs_0_, bf16[128,2048]{1,0:T(8,128)(2,1)} %get-tuple-element.16.refs_1_, ...), custom_call_target="tpu_custom_call" | custom-call | tf_op jit(solution)/shard_map/pallas_call | solution.py:610
